TPU v7x, 32 devices: a whole 2x2x4 slice. The times are simulated.
32 devices in a mesh: row: 4 (over y, x), col: 4 (over z), depth: 2 (over core).
Axes of the slice: x: 2, y: 2, z: 4, core: 2. Of those that a mesh axis runs over, the one named last changes fastest.
Arguments:
- left_block_slots: bfloat16 [4, 4, 2, 1, 16, 128, 128], P('row', 'col', 'depth'), may hold values from -6 to 6
- a_index: int32 [4, 4, 2, 1, 16], P('row', 'col', 'depth'), may hold values from 0 to 31, as said below
- a_count: int32 [4, 4, 2, 1], P('row', 'col', 'depth'), may hold values from 4 to 16, as said below
- b_blocks: bfloat16 [4, 4, 2, 1, 8, 128, 128], P('row', 'col', 'depth'), may hold values from -0.1875 to 0.1875
- b_index: int32 [4, 4, 2, 1, 8], P('row', 'col', 'depth'), may hold values from 0 to 63, as said below
- b_count: int32 [4, 4, 2, 1], P('row', 'col', 'depth'), may hold values from 2 to 8, as said below
- c_index: int32 [4, 4, 24], P('row', 'col'), may hold values from 0 to 31, as said below
Outputs:
- c_blocks: bfloat16 [4, 4, 24, 128, 128], P('row', 'col', 'depth')
Inputs may be any that keep to these rules, and one draw needn't show every extreme that they name: `a_index`: within one panel the live positions are distinct. `a_count`: some panel has all 16 slots live. `b_index`: within one panel the live positions are distinct. `b_count`: some panel has all 8 slots live. `c_index`: within one panel the positions are distinct.
All inputs are finite; a program needn't handle non-finite values.
Results may differ from a plain program's by a relative error of at most 0.001.
Values may be sent and summed in bfloat16 or wider, within the bound.
A program may use at most 128 MiB of HBM per device.

v0:
```python
import jax
import jax.numpy as jnp
from jax import lax
from jax.sharding import PartitionSpec as P

KB = 8
CB = 8


def from_behind(value, axis, steps):
    count = lax.axis_size(axis)
    pairs = [(source, (source + steps) % count) for source in range(count)]
    return lax.ppermute(value, axis, pairs)


def select_blocks(blocks, positions, count, wanted):
    slots = blocks.shape[0]
    side = blocks.shape[-1]
    live = jnp.arange(slots, dtype=jnp.int32) < count
    picker = ((wanted.reshape(-1)[:, None] == positions[None, :]) & live[None, :]).astype(
        jnp.bfloat16
    )
    flat = blocks.reshape(slots, side * side)
    chosen = jnp.dot(picker, flat, preferred_element_type=jnp.float32).astype(jnp.bfloat16)
    return chosen.reshape(wanted.shape + (side, side))


def contribute(product_total, left_portion, b_part, left_pick, right_pick):
    left_strip = select_blocks(left_portion[0], left_portion[1], left_portion[2], left_pick)
    right_strip = select_blocks(b_part[0], b_part[1], b_part[2], right_pick)
    return product_total + jnp.einsum(
        "oxmn,oxnw->omw", left_strip, right_strip, preferred_element_type=jnp.float32
    )


def pick(held, index):
    return tuple((lax.dynamic_index_in_dim(member, index, 0, keepdims=False) for member in held))


def window(held, leading, slot_count):
    chosen = jnp.stack(
        [
            jnp.asarray(leading, jnp.int32) % slot_count,
            (jnp.asarray(leading, jnp.int32) + 1) % slot_count,
        ]
    )
    return tuple((jnp.take(member, chosen, axis=0) for member in held))


def body(left_block_slots, a_index, a_count, b_blocks, b_index, b_count, c_index):
    row_pos = lax.axis_index("row")
    n_row = lax.axis_size("row")
    n_col = lax.axis_size("col")
    span = max(n_row, n_col)
    a_slots = left_block_slots.shape[3]
    b_slots = b_blocks.shape[3]
    rounds = max(a_slots, b_slots)
    length = span // rounds
    targets = c_index[0, 0]
    rows_t = targets // CB
    cols_t = targets % CB
    inner_cols = jnp.arange(KB, dtype=jnp.int32)
    left_pick = rows_t[:, None] * KB + inner_cols[None, :]
    right_pick = inner_cols[None, :] * CB + cols_t[:, None]
    a_held = (left_block_slots[0, 0, 0], a_index[0, 0, 0], a_count[0, 0, 0])
    b_held = (b_blocks[0, 0, 0], b_index[0, 0, 0], b_count[0, 0, 0])

    def a_use(held):
        return pick(held, 0)

    def a_move(held):
        return tuple(from_behind((held[0], held[1], held[2]), "col", -1))

    def a_end(held):
        return a_move(held)

    def b_begin(held, rnd):
        if b_slots > 1:
            return window(b_held, rnd, b_slots)
        return held

    def b_use(held, step):
        if b_slots > 1:
            return pick(held, (row_pos + step) // n_row)
        return pick(held, 0)

    def right_shifted(held):
        return tuple(from_behind((held[0], held[1], held[2]), "row", -1))

    def b_end(held):
        if b_slots == 1:
            return right_shifted(held)
        return held

    b_start = b_begin(b_held, 0)

    def run_round(rnd, a_now, b_now, product_total):
        a_now = tuple(a_now)
        b_now = tuple(b_begin(b_now, rnd))

        def inner(step, carry):
            a_cur, b_cur, acc = carry
            acc = contribute(acc, a_use(a_cur), b_use(b_cur, step), left_pick, right_pick)
            return (tuple(a_move(a_cur)), tuple(right_shifted(b_cur)), acc)

        a_now, b_now, product_total = lax.fori_loop(
            0, length - 1, inner, (a_now, b_now, product_total)
        )
        product_total = contribute(
            product_total, a_use(a_now), b_use(b_now, length - 1), left_pick, right_pick
        )
        return (a_now, b_now, product_total)

    def full_round(rnd, carry):
        a_now, b_now, product_total = run_round(rnd, carry[0], carry[1], carry[2])
        return (tuple(a_end(a_now)), tuple(b_end(b_now)), product_total)

    side = left_block_slots.shape[-1]
    start = jnp.zeros((targets.shape[0], side, side), jnp.float32)
    a_last, b_last, product_total = lax.fori_loop(
        0, rounds - 1, full_round, (tuple(a_held), tuple(b_start), start)
    )
    a_last, b_last, product_total = run_round(rounds - 1, a_last, b_last, product_total)
    shares = lax.psum_scatter(product_total, "depth", scatter_dimension=0, tiled=True)
    return shares.astype(jnp.bfloat16)[None, None]


def solution(mesh):
    placed = (
        P("row", "col", "depth", None, None, None, None),
        P("row", "col", "depth", None, None),
        P("row", "col", "depth", None),
        P("row", "col", "depth", None, None, None, None),
        P("row", "col", "depth", None, None),
        P("row", "col", "depth", None),
        P("row", "col", None),
    )
    return jax.shard_map(
        body,
        mesh=mesh,
        in_specs=placed,
        out_specs=P("row", "col", "depth", None, None),
        check_vma=False,
    )
```

profile of v0, /device:TPU:0, one launch (start us, length us, event | category | flops | bytes accessed | tf_op | source)
XLA Modules:
  0.0 168.5 jit_solution(2110988298738970266)
XLA Ops:
  6.5 1.0 copy.84
  7.6 0.9 copy.86
  12.5 116.8 %while.23 = (s32[]{:T(128)}, bf16[1,16,128,128]{3,2,1,0:T(8,128)(2,1)S(1)}, s32[1,16]{1,0:T(1,128)S(1)}, s32[1]{0:T(128)}, bf16[1,8,128,128]{3,2,1,0:T(8,128)(2,...) while((s32[]{:T(128)}, ...), condition=%wide.region_1.2_spmd.clone, body=%wide.region_0.1_spmd.clone.sunk | while | flops 963388800 | bytes 33824092 | solution.py:106
  12.5 5.1 %collective-permute-start = (bf16[1,16,128,128]{3,2,1,0:T(8,128)(2,1)S(1)}, bf16[1,16,128,128]{3,2,1,0:T(8,128)(2,1)S(1)}, u32[]{:S(2)}, u32[]{:S(2)}) collective-permute-start(bf16[1,16,128,128]{3,2,1,0:T(8,128)(2,1)S(1)} %copy.61), channel_id=1, source_target_pairs={{0,6},{2,0},{4,2},{6,4},{1,7},{3,1},{5,3},{7,5},{8,14},{10,8},{12,... | collective-permute-start | bytes 1572872 | tf_op jit(solution)/shard_map/while/body/eval_jaxpr/ppermute | solution.py:13
  17.7 2.5 %collective-permute-start.3 = (bf16[1,8,128,128]{3,2,1,0:T(8,128)(2,1)S(1)}, bf16[1,8,128,128]{3,2,1,0:T(8,128)(2,1)S(1)}, u32[]{:S(2)}, u32[]{:S(2)}) collective-permute-start(bf16[1,8,128,128]{3,2,1,0:T(8,128)(2,1)S(1)} %copy.64), channel_id=1, source_target_pairs={{0,24},{8,0},{16,8},{24,16},{1,25},{9,1},{17,9},{25,17},{2,26},{10... | collective-permute-start | bytes 786440 | tf_op jit(solution)/shard_map/while/body/eval_jaxpr/ppermute | solution.py:13
  20.6 8.3 %collective-permute-start.2 = (s32[1]{0:T(128)}, s32[1]{0:T(128)}, u32[]{:S(2)}, u32[]{:S(2)}) collective-permute-start(s32[1]{0:T(128)} %copy.63), channel_id=1, source_target_pairs={{0,6},{2,0},{4,2},{6,4},{1,7},{3,1},{5,3},{7,5},{8,14},{10,8},{12,... | collective-permute-start | bytes 20 | tf_op jit(solution)/shard_map/while/body/eval_jaxpr/ppermute | solution.py:13
  28.9 2.4 %collective-permute-start.4 = (s32[1,8]{1,0:T(1,128)S(1)}, s32[1,8]{1,0:T(1,128)S(1)}, u32[]{:S(2)}, u32[]{:S(2)}) collective-permute-start(s32[1,8]{1,0:T(1,128)S(1)} %copy.65), channel_id=1, source_target_pairs={{0,24},{8,0},{16,8},{24,16},{1,25},{9,1},{17,9},{25,17},{2,26},{10... | collective-permute-start | bytes 104 | tf_op jit(solution)/shard_map/while/body/eval_jaxpr/ppermute | solution.py:13
  31.5 4.5 %fusion.72 = bf16[24,8,128,128]{3,1,2,0:T(8,128)(2,1)} fusion(bf16[2,8,128,128]{3,2,1,0:T(8,128)(2,1)S(1)} %bitcast.99, s32[16]{0:T(128)S(1)} %bitcast.103, s32[192]{0:T(256)S(1)} %eq.152, pred[16]{0:T(512)(128)(4,1)S(1)} %iota_compare_fusion.6), kind=kOutput, calls=%fused_computation.6.clone.1 | convolution fusion | flops 103815168 | bytes 6816592 | tf_op jit(solution)/shard_map/while/body/eval_jaxpr/dot_general | solution.py:24
  36.0 9.4 %copy.51 = bf16[24,8,128,128]{2,1,3,0:T(8,128)(2,1)} copy(bf16[24,8,128,128]{3,1,2,0:T(8,128)(2,1)} %fusion.72) | data formatting | bytes 12582912 | tf_op jit(solution)/shard_map/while/body/eval_jaxpr/reshape | solution.py:25
  45.5 6.9 %bitcast_add_fusion.3 = f32[24,128,128]{2,1,0:T(8,128)S(1)} fusion(f32[24,128,128]{2,1,0:T(8,128)S(1)} %get-tuple-element.232, bf16[24,8,128,128]{2,1,3,0:T(8,128)(2,1)} %copy.51, pred[]{:T(512)S(6)} %compare.14, bf16[1,8,128,128]{3,2,1,0:T(8,128)(2,1)S(1)} %copy.64, s32[8]{0:T(128)S(1)} %bitcast.106, s32[192]{0:T(256)S(1)} %eq.153, ...), kind=kOutput, calls=%fused_computation.7.clone.1 | convolution fusion | flops 859573248 | bytes 9700137 | tf_op jit(solution)/shard_map/while/body/eval_jaxpr/oxmn,oxnw->omw/dot_general | solution.py:31
  52.4 1.9 %collective-permute-start.5 = (s32[1]{0:T(128)}, s32[1]{0:T(128)}, u32[]{:S(2)}, u32[]{:S(2)}) collective-permute-start(s32[1]{0:T(128)} %copy.66), channel_id=1, source_target_pairs={{0,24},{8,0},{16,8},{24,16},{1,25},{9,1},{17,9},{25,17},{2,26},{10... | collective-permute-start | bytes 20 | tf_op jit(solution)/shard_map/while/body/eval_jaxpr/ppermute | solution.py:13
  54.3 1.7 collective-permute-done.5
  57.9 1.5 collective-permute-start.3
  59.9 7.1 %collective-permute-start.2 = (s32[1]{0:T(128)}, s32[1]{0:T(128)}, u32[]{:S(2)}, u32[]{:S(2)}) collective-permute-start(s32[1]{0:T(128)} %copy.63), channel_id=1, source_target_pairs={{0,6},{2,0},{4,2},{6,4},{1,7},{3,1},{5,3},{7,5},{8,14},{10,8},{12,... | collective-permute-start | bytes 20 | tf_op jit(solution)/shard_map/while/body/eval_jaxpr/ppermute | solution.py:13
  67.0 1.4 collective-permute-start.4
  68.6 4.5 %fusion.72 = bf16[24,8,128,128]{3,1,2,0:T(8,128)(2,1)} fusion(bf16[2,8,128,128]{3,2,1,0:T(8,128)(2,1)S(1)} %bitcast.99, s32[16]{0:T(128)S(1)} %bitcast.103, s32[192]{0:T(256)S(1)} %eq.152, pred[16]{0:T(512)(128)(4,1)S(1)} %iota_compare_fusion.6), kind=kOutput, calls=%fused_computation.6.clone.1 | convolution fusion | flops 103815168 | bytes 6816592 | tf_op jit(solution)/shard_map/while/body/eval_jaxpr/dot_general | solution.py:24
  73.1 9.4 %copy.51 = bf16[24,8,128,128]{2,1,3,0:T(8,128)(2,1)} copy(bf16[24,8,128,128]{3,1,2,0:T(8,128)(2,1)} %fusion.72) | data formatting | bytes 12582912 | tf_op jit(solution)/shard_map/while/body/eval_jaxpr/reshape | solution.py:25
  82.6 6.9 %bitcast_add_fusion.3 = f32[24,128,128]{2,1,0:T(8,128)S(1)} fusion(f32[24,128,128]{2,1,0:T(8,128)S(1)} %get-tuple-element.232, bf16[24,8,128,128]{2,1,3,0:T(8,128)(2,1)} %copy.51, pred[]{:T(512)S(6)} %compare.14, bf16[1,8,128,128]{3,2,1,0:T(8,128)(2,1)S(1)} %copy.64, s32[8]{0:T(128)S(1)} %bitcast.106, s32[192]{0:T(256)S(1)} %eq.153, ...), kind=kOutput, calls=%fused_computation.7.clone.1 | convolution fusion | flops 859573248 | bytes 9700137 | tf_op jit(solution)/shard_map/while/body/eval_jaxpr/oxmn,oxnw->omw/dot_general | solution.py:31
  89.5 1.9 %collective-permute-start.5 = (s32[1]{0:T(128)}, s32[1]{0:T(128)}, u32[]{:S(2)}, u32[]{:S(2)}) collective-permute-start(s32[1]{0:T(128)} %copy.66), channel_id=1, source_target_pairs={{0,24},{8,0},{16,8},{24,16},{1,25},{9,1},{17,9},{25,17},{2,26},{10... | collective-permute-start | bytes 20 | tf_op jit(solution)/shard_map/while/body/eval_jaxpr/ppermute | solution.py:13
  91.4 1.7 collective-permute-done.5
  95.0 1.5 collective-permute-start.3
  96.9 4.9 %collective-permute-start.2 = (s32[1]{0:T(128)}, s32[1]{0:T(128)}, u32[]{:S(2)}, u32[]{:S(2)}) collective-permute-start(s32[1]{0:T(128)} %copy.63), channel_id=1, source_target_pairs={{0,6},{2,0},{4,2},{6,4},{1,7},{3,1},{5,3},{7,5},{8,14},{10,8},{12,... | collective-permute-start | bytes 20 | tf_op jit(solution)/shard_map/while/body/eval_jaxpr/ppermute | solution.py:13
  101.9 1.4 collective-permute-start.4
  103.5 4.5 %fusion.72 = bf16[24,8,128,128]{3,1,2,0:T(8,128)(2,1)} fusion(bf16[2,8,128,128]{3,2,1,0:T(8,128)(2,1)S(1)} %bitcast.99, s32[16]{0:T(128)S(1)} %bitcast.103, s32[192]{0:T(256)S(1)} %eq.152, pred[16]{0:T(512)(128)(4,1)S(1)} %iota_compare_fusion.6), kind=kOutput, calls=%fused_computation.6.clone.1 | convolution fusion | flops 103815168 | bytes 6816592 | tf_op jit(solution)/shard_map/while/body/eval_jaxpr/dot_general | solution.py:24
  108.0 9.4 %copy.51 = bf16[24,8,128,128]{2,1,3,0:T(8,128)(2,1)} copy(bf16[24,8,128,128]{3,1,2,0:T(8,128)(2,1)} %fusion.72) | data formatting | bytes 12582912 | tf_op jit(solution)/shard_map/while/body/eval_jaxpr/reshape | solution.py:25
  117.5 6.9 %bitcast_add_fusion.3 = f32[24,128,128]{2,1,0:T(8,128)S(1)} fusion(f32[24,128,128]{2,1,0:T(8,128)S(1)} %get-tuple-element.232, bf16[24,8,128,128]{2,1,3,0:T(8,128)(2,1)} %copy.51, pred[]{:T(512)S(6)} %compare.14, bf16[1,8,128,128]{3,2,1,0:T(8,128)(2,1)S(1)} %copy.64, s32[8]{0:T(128)S(1)} %bitcast.106, s32[192]{0:T(256)S(1)} %eq.153, ...), kind=kOutput, calls=%fused_computation.7.clone.1 | convolution fusion | flops 859573248 | bytes 9700137 | tf_op jit(solution)/shard_map/while/body/eval_jaxpr/oxmn,oxnw->omw/dot_general | solution.py:31
  124.4 2.8 %collective-permute-start.5 = (s32[1]{0:T(128)}, s32[1]{0:T(128)}, u32[]{:S(2)}, u32[]{:S(2)}) collective-permute-start(s32[1]{0:T(128)} %copy.66), channel_id=1, source_target_pairs={{0,24},{8,0},{16,8},{24,16},{1,25},{9,1},{17,9},{25,17},{2,26},{10... | collective-permute-start | bytes 20 | tf_op jit(solution)/shard_map/while/body/eval_jaxpr/ppermute | solution.py:13
  129.4 4.5 %fusion.32 = bf16[24,8,128,128]{3,1,2,0:T(8,128)(2,1)} fusion(bf16[2,8,128,128]{3,2,1,0:T(8,128)(2,1)S(1)} %bitcast.101, s32[16]{0:T(128)S(1)} %bitcast.105, s32[192]{0:T(256)S(1)} %add.90, pred[16]{0:T(512)(128)(4,1)S(1)} %iota_compare_fusion.3), kind=kOutput, calls=%fused_computation.30 | convolution fusion | flops 103815168 | bytes 6816592 | tf_op jit(solution)/shard_map/dot_general | solution.py:24
  133.9 9.4 %copy.19 = bf16[24,8,128,128]{2,1,3,0:T(8,128)(2,1)} copy(bf16[24,8,128,128]{3,1,2,0:T(8,128)(2,1)} %fusion.32) | data formatting | bytes 12582912 | tf_op jit(solution)/shard_map/reshape | solution.py:25
  143.5 7.7 %bitcast_add_fusion.1 = f32[24,128,128]{2,1,0:T(8,128)} fusion(f32[24,128,128]{2,1,0:T(8,128)S(1)} %get-tuple-element.63, bf16[24,8,128,128]{2,1,3,0:T(8,128)(2,1)} %copy.19, bf16[1,8,128,128]{3,2,1,0:T(8,128)(2,1)S(1)} %get-tuple-element.69, s32[8]{0:T(128)S(1)} %bitcast.108, s32[192]{0:T(256)S(1)} %add.91, pred[8]{0:T(512)(128)(4,1)S(1)} %iota_compare_fusion.2), kind=kOutput, calls=%fused_computation.31 | convolution fusion | flops 859180032 | bytes 9700136 | tf_op jit(solution)/shard_map/oxmn,oxnw->omw/dot_general | solution.py:31
  151.1 8.5 %reduce-scatter.2.cloned.1.call-done = f32[12,128,128]{2,1,0:T(8,128)} async-done(((f32[24,128,128]{2,1,0:T(8,128)}), f32[12,128,128]{2,1,0:T(8,128)}) %reduce-scatter.2.cloned.1.call-update) | async-done | bytes 786448 | tf_op jit(solution)/shard_map/reduce_scatter | solution.py:124
  159.7 1.9 %convert_bitcast_fusion = bf16[1,1,12,128,128]{4,3,2,1,0:T(8,128)(2,1)} fusion(f32[12,128,128]{2,1,0:T(8,128)} %reduce-scatter.2.cloned.1.call-done), kind=kLoop, calls=%fused_computation.34 | loop fusion | flops 196608 | bytes 1179648 | tf_op jit(solution)/shard_map/broadcast_in_dim | solution.py:125
  (64 shorter events, 6.9 us)
Async XLA Ops:
  6.5 153.1 %reduce-scatter.2.cloned.1.call-start = ((), (), s32[]{:S(2)}) async-start(), calls=%async_computation.1 | async-start | bytes 2359296 | tf_op jit(solution)/shard_map/reduce_scatter | solution.py:124
  12.5 116.9 %copy-start.1 = (s32[24,8]{1,0:T(8,128)S(1)}, s32[24,8]{1,0:T(8,128)}, u32[]{:S(2)}) copy-start(s32[24,8]{1,0:T(8,128)} %get-tuple-element.139) | copy-start | bytes 2308
  12.5 43.5 %collective-permute-start = (bf16[1,16,128,128]{3,2,1,0:T(8,128)(2,1)S(1)}, bf16[1,16,128,128]{3,2,1,0:T(8,128)(2,1)S(1)}, u32[]{:S(2)}, u32[]{:S(2)}) collective-permute-start(bf16[1,16,128,128]{3,2,1,0:T(8,128)(2,1)S(1)} %copy.61), channel_id=1, source_target_pairs={{0,6},{2,0},{4,2},{6,4},{1,7},{3,1},{5,3},{7,5},{8,14},{10,8},{12,... | collective-permute-start | bytes 1572872 | tf_op jit(solution)/shard_map/while/body/eval_jaxpr/ppermute | solution.py:13
  17.7 38.3 %collective-permute-start.3 = (bf16[1,8,128,128]{3,2,1,0:T(8,128)(2,1)S(1)}, bf16[1,8,128,128]{3,2,1,0:T(8,128)(2,1)S(1)}, u32[]{:S(2)}, u32[]{:S(2)}) collective-permute-start(bf16[1,8,128,128]{3,2,1,0:T(8,128)(2,1)S(1)} %copy.64), channel_id=1, source_target_pairs={{0,24},{8,0},{16,8},{24,16},{1,25},{9,1},{17,9},{25,17},{2,26},{10... | collective-permute-start | bytes 786440 | tf_op jit(solution)/shard_map/while/body/eval_jaxpr/ppermute | solution.py:13
  20.2 35.8 %collective-permute-start.1 = (s32[1,16]{1,0:T(1,128)S(1)}, s32[1,16]{1,0:T(1,128)S(1)}, u32[]{:S(2)}, u32[]{:S(2)}) collective-permute-start(s32[1,16]{1,0:T(1,128)S(1)} %copy.62), channel_id=1, source_target_pairs={{0,6},{2,0},{4,2},{6,4},{1,7},{3,1},{5,3},{7,5},{8,14},{10,8},{12,... | collective-permute-start | bytes 200 | tf_op jit(solution)/shard_map/while/body/eval_jaxpr/ppermute | solution.py:13
  20.6 31.8 %collective-permute-start.2 = (s32[1]{0:T(128)}, s32[1]{0:T(128)}, u32[]{:S(2)}, u32[]{:S(2)}) collective-permute-start(s32[1]{0:T(128)} %copy.63), channel_id=1, source_target_pairs={{0,6},{2,0},{4,2},{6,4},{1,7},{3,1},{5,3},{7,5},{8,14},{10,8},{12,... | collective-permute-start | bytes 20 | tf_op jit(solution)/shard_map/while/body/eval_jaxpr/ppermute | solution.py:13
  28.9 27.1 %collective-permute-start.4 = (s32[1,8]{1,0:T(1,128)S(1)}, s32[1,8]{1,0:T(1,128)S(1)}, u32[]{:S(2)}, u32[]{:S(2)}) collective-permute-start(s32[1,8]{1,0:T(1,128)S(1)} %copy.65), channel_id=1, source_target_pairs={{0,24},{8,0},{16,8},{24,16},{1,25},{9,1},{17,9},{25,17},{2,26},{10... | collective-permute-start | bytes 104 | tf_op jit(solution)/shard_map/while/body/eval_jaxpr/ppermute | solution.py:13
  52.4 3.5 %collective-permute-start.5 = (s32[1]{0:T(128)}, s32[1]{0:T(128)}, u32[]{:S(2)}, u32[]{:S(2)}) collective-permute-start(s32[1]{0:T(128)} %copy.66), channel_id=1, source_target_pairs={{0,24},{8,0},{16,8},{24,16},{1,25},{9,1},{17,9},{25,17},{2,26},{10... | collective-permute-start | bytes 20 | tf_op jit(solution)/shard_map/while/body/eval_jaxpr/ppermute | solution.py:13
  57.4 35.7 %collective-permute-start = (bf16[1,16,128,128]{3,2,1,0:T(8,128)(2,1)S(1)}, bf16[1,16,128,128]{3,2,1,0:T(8,128)(2,1)S(1)}, u32[]{:S(2)}, u32[]{:S(2)}) collective-permute-start(bf16[1,16,128,128]{3,2,1,0:T(8,128)(2,1)S(1)} %copy.61), channel_id=1, source_target_pairs={{0,6},{2,0},{4,2},{6,4},{1,7},{3,1},{5,3},{7,5},{8,14},{10,8},{12,... | collective-permute-start | bytes 1572872 | tf_op jit(solution)/shard_map/while/body/eval_jaxpr/ppermute | solution.py:13
  57.9 35.2 %collective-permute-start.3 = (bf16[1,8,128,128]{3,2,1,0:T(8,128)(2,1)S(1)}, bf16[1,8,128,128]{3,2,1,0:T(8,128)(2,1)S(1)}, u32[]{:S(2)}, u32[]{:S(2)}) collective-permute-start(bf16[1,8,128,128]{3,2,1,0:T(8,128)(2,1)S(1)} %copy.64), channel_id=1, source_target_pairs={{0,24},{8,0},{16,8},{24,16},{1,25},{9,1},{17,9},{25,17},{2,26},{10... | collective-permute-start | bytes 786440 | tf_op jit(solution)/shard_map/while/body/eval_jaxpr/ppermute | solution.py:13
  59.4 33.7 %collective-permute-start.1 = (s32[1,16]{1,0:T(1,128)S(1)}, s32[1,16]{1,0:T(1,128)S(1)}, u32[]{:S(2)}, u32[]{:S(2)}) collective-permute-start(s32[1,16]{1,0:T(1,128)S(1)} %copy.62), channel_id=1, source_target_pairs={{0,6},{2,0},{4,2},{6,4},{1,7},{3,1},{5,3},{7,5},{8,14},{10,8},{12,... | collective-permute-start | bytes 200 | tf_op jit(solution)/shard_map/while/body/eval_jaxpr/ppermute | solution.py:13
  59.9 29.7 %collective-permute-start.2 = (s32[1]{0:T(128)}, s32[1]{0:T(128)}, u32[]{:S(2)}, u32[]{:S(2)}) collective-permute-start(s32[1]{0:T(128)} %copy.63), channel_id=1, source_target_pairs={{0,6},{2,0},{4,2},{6,4},{1,7},{3,1},{5,3},{7,5},{8,14},{10,8},{12,... | collective-permute-start | bytes 20 | tf_op jit(solution)/shard_map/while/body/eval_jaxpr/ppermute | solution.py:13
  67.0 26.1 %collective-permute-start.4 = (s32[1,8]{1,0:T(1,128)S(1)}, s32[1,8]{1,0:T(1,128)S(1)}, u32[]{:S(2)}, u32[]{:S(2)}) collective-permute-start(s32[1,8]{1,0:T(1,128)S(1)} %copy.65), channel_id=1, source_target_pairs={{0,24},{8,0},{16,8},{24,16},{1,25},{9,1},{17,9},{25,17},{2,26},{10... | collective-permute-start | bytes 104 | tf_op jit(solution)/shard_map/while/body/eval_jaxpr/ppermute | solution.py:13
  89.5 3.5 %collective-permute-start.5 = (s32[1]{0:T(128)}, s32[1]{0:T(128)}, u32[]{:S(2)}, u32[]{:S(2)}) collective-permute-start(s32[1]{0:T(128)} %copy.66), channel_id=1, source_target_pairs={{0,24},{8,0},{16,8},{24,16},{1,25},{9,1},{17,9},{25,17},{2,26},{10... | collective-permute-start | bytes 20 | tf_op jit(solution)/shard_map/while/body/eval_jaxpr/ppermute | solution.py:13
  94.5 33.5 %collective-permute-start = (bf16[1,16,128,128]{3,2,1,0:T(8,128)(2,1)S(1)}, bf16[1,16,128,128]{3,2,1,0:T(8,128)(2,1)S(1)}, u32[]{:S(2)}, u32[]{:S(2)}) collective-permute-start(bf16[1,16,128,128]{3,2,1,0:T(8,128)(2,1)S(1)} %copy.61), channel_id=1, source_target_pairs={{0,6},{2,0},{4,2},{6,4},{1,7},{3,1},{5,3},{7,5},{8,14},{10,8},{12,... | collective-permute-start | bytes 1572872 | tf_op jit(solution)/shard_map/while/body/eval_jaxpr/ppermute | solution.py:13
  95.0 33.0 %collective-permute-start.3 = (bf16[1,8,128,128]{3,2,1,0:T(8,128)(2,1)S(1)}, bf16[1,8,128,128]{3,2,1,0:T(8,128)(2,1)S(1)}, u32[]{:S(2)}, u32[]{:S(2)}) collective-permute-start(bf16[1,8,128,128]{3,2,1,0:T(8,128)(2,1)S(1)} %copy.64), channel_id=1, source_target_pairs={{0,24},{8,0},{16,8},{24,16},{1,25},{9,1},{17,9},{25,17},{2,26},{10... | collective-permute-start | bytes 786440 | tf_op jit(solution)/shard_map/while/body/eval_jaxpr/ppermute | solution.py:13
  96.5 31.5 %collective-permute-start.1 = (s32[1,16]{1,0:T(1,128)S(1)}, s32[1,16]{1,0:T(1,128)S(1)}, u32[]{:S(2)}, u32[]{:S(2)}) collective-permute-start(s32[1,16]{1,0:T(1,128)S(1)} %copy.62), channel_id=1, source_target_pairs={{0,6},{2,0},{4,2},{6,4},{1,7},{3,1},{5,3},{7,5},{8,14},{10,8},{12,... | collective-permute-start | bytes 200 | tf_op jit(solution)/shard_map/while/body/eval_jaxpr/ppermute | solution.py:13
  96.9 27.5 %collective-permute-start.2 = (s32[1]{0:T(128)}, s32[1]{0:T(128)}, u32[]{:S(2)}, u32[]{:S(2)}) collective-permute-start(s32[1]{0:T(128)} %copy.63), channel_id=1, source_target_pairs={{0,6},{2,0},{4,2},{6,4},{1,7},{3,1},{5,3},{7,5},{8,14},{10,8},{12,... | collective-permute-start | bytes 20 | tf_op jit(solution)/shard_map/while/body/eval_jaxpr/ppermute | solution.py:13
  101.9 26.1 %collective-permute-start.4 = (s32[1,8]{1,0:T(1,128)S(1)}, s32[1,8]{1,0:T(1,128)S(1)}, u32[]{:S(2)}, u32[]{:S(2)}) collective-permute-start(s32[1,8]{1,0:T(1,128)S(1)} %copy.65), channel_id=1, source_target_pairs={{0,24},{8,0},{16,8},{24,16},{1,25},{9,1},{17,9},{25,17},{2,26},{10... | collective-permute-start | bytes 104 | tf_op jit(solution)/shard_map/while/body/eval_jaxpr/ppermute | solution.py:13
  124.4 3.5 %collective-permute-start.5 = (s32[1]{0:T(128)}, s32[1]{0:T(128)}, u32[]{:S(2)}, u32[]{:S(2)}) collective-permute-start(s32[1]{0:T(128)} %copy.66), channel_id=1, source_target_pairs={{0,24},{8,0},{16,8},{24,16},{1,25},{9,1},{17,9},{25,17},{2,26},{10... | collective-permute-start | bytes 20 | tf_op jit(solution)/shard_map/while/body/eval_jaxpr/ppermute | solution.py:13
  133.9 9.5 %copy-start = (s32[24,8]{1,0:T(8,128)S(1)}, s32[24,8]{1,0:T(8,128)}, u32[]{:S(2)}) copy-start(s32[24,8]{1,0:T(8,128)} %get-tuple-element.140) | copy-start | bytes 2308
Sparse Core Ops, SparseCore 0:
  151.3 8.3 reduce-scatter.1
where the time goes:
time: 170 us; the launch traced here: 168 us
  matrix products  46.3 us (27%)
  starting transfers between devices  45.2 us (27%)
  local copies, waits for them, and re-layouts  41.9 us (25%)
  between operations  14.7 us (9%)
  waiting for transfers between devices  12.6 us (7%)
  loops' own time  4.2 us (2%)
  other arithmetic  3.55 us (2%)
    ppermute x18, starting transfers between devices, from_behind(): return lax.ppermute(value, axis, pairs)  45.2 us
    reshape x4, local copies, waits for them, and re-layouts, select_blocks(): return chosen.reshape(wanted.shape + (side, side))  37.7 us
    dot_general x4, matrix products, contribute(): jnp.einsum('oxmn,oxnw->omw', left_strip, right_strip, preferred_element_t...  28.4 us
    dot_general x4, matrix products, select_blocks(): jnp.dot(picker, flat, preferred_element_type=jnp.float32)  17.9 us
    reduce_scatter x1, waiting for transfers between devices, body(): lax.psum_scatter(product_total, 'depth', scatter_dimension=0, tiled=True)  8.52 us
    another operation x1, loops' own time, run_round(): lax.fori_loop(0, length - 1, inner, (a_now, b_now, product_total))  4.2 us
    ppermute x18, waiting for transfers between devices, from_behind(): return lax.ppermute(value, axis, pairs)  4.06 us
  transfers between devices with their start and end apart: 19, of which 4 were waited for; matrix products, arithmetic and copies ran while one was open for 38% of the time, Pallas kernels for 0%

commit v1 on v0

--- a/solution.py
+++ b/solution.py
@@ -1,10 +1,15 @@
 import jax
 import jax.numpy as jnp
 from jax import lax
+from jax.experimental import pallas as pl
+from jax.experimental.pallas import tpu as pltpu
 from jax.sharding import PartitionSpec as P
 
+RB = 4
 KB = 8
 CB = 8
+NCH = 4
+MESH = pl.DeviceIdType.MESH
 
 
 def from_behind(value, axis, steps):
@@ -125,6 +130,337 @@
     return shares.astype(jnp.bfloat16)[None, None]
 
 
+def fast_kernel(
+    a_hbm, b_hbm, a_idx, a_cnt, b_idx, b_cnt, c_idx, out,
+    own, low_one, high_one, two, far_parts, b_all, tab_a, tab_b, ind_a, ind_b, b_dense, a_dense, total, give, take,
+    local_sem, ind_sem, a_send, a_recv, b_send, b_recv,
+    ta_send, ta_recv, tb_send, tb_recv, x_send, x_recv,
+):
+    r = lax.axis_index("row")
+    c = lax.axis_index("col")
+    d = lax.axis_index("depth")
+    n = 4
+    slots_a, side = a_hbm.shape[0], a_hbm.shape[1]
+    slots_b = b_hbm.shape[0]
+    half_b = slots_b // 2
+    rows = side // NCH
+    mine = out.shape[0]
+    x, y = r % 2, r // 2
+    across = (y * 2 + (1 - x), (1 - y) * 2 + x)
+    corner = (1 - y) * 2 + (1 - x)
+
+    barrier = pltpu.get_barrier_semaphore()
+    z_peers = [(c + s) % n for s in range(1, n)]
+    r_peers = [(r + s) % n for s in range(1, n)]
+    for z in z_peers:
+        pl.semaphore_signal(barrier, inc=1, device_id=(r, z, d), device_id_type=MESH)
+    for q in r_peers:
+        pl.semaphore_signal(barrier, inc=1, device_id=(q, c, d), device_id_type=MESH)
+    pl.semaphore_signal(barrier, inc=1, device_id=(r, c, 1 - d), device_id_type=MESH)
+
+    load_a = pltpu.make_async_copy(a_hbm, own.at[pl.ds(0, slots_a)], local_sem.at[0])
+    load_b = pltpu.make_async_copy(b_hbm, b_all.at[r, pl.ds(0, slots_b)], local_sem.at[1])
+    load_a.start()
+    load_b.start()
+
+    lane = lax.broadcasted_iota(jnp.int32, (8, 128), 1)
+    inv_a = jnp.full((8, 128), slots_a, jnp.int32)
+    for s in range(slots_a):
+        inv_a = jnp.where((lane == a_idx[s]) & (s < a_cnt[0]), s, inv_a)
+    inv_b = jnp.full((8, 128), slots_b, jnp.int32)
+    for s in range(slots_b):
+        inv_b = jnp.where((lane == b_idx[s]) & (s < b_cnt[0]), s, inv_b)
+    tab_a[c] = inv_a
+    tab_b[r] = inv_b
+    for p in range(n):
+        b_all[p, slots_b] = jnp.zeros((side, side), b_all.dtype)
+    for panel_ref in (own, low_one, high_one, two):
+        panel_ref[slots_a] = jnp.zeros((side, side), panel_ref.dtype)
+    for part_ref in far_parts:
+        part_ref[slots_a] = jnp.zeros((rows, side), part_ref.dtype)
+
+    def zero(t, carry):
+        total[t] = jnp.zeros((side, side), jnp.float32)
+        return carry
+
+    lax.fori_loop(0, RB * CB, zero, 0)
+
+    held = ((own, low_one, two), (own, high_one, two))
+
+    def piece(way, delta, h):
+        if delta == n - 1:
+            return far_parts[h].at[pl.ds(0, slots_a)]
+        return held[way][delta].at[pl.ds(0, slots_a), pl.ds(h * rows, rows)]
+
+    def a_copy(way, delta, h):
+        return pltpu.make_async_remote_copy(
+            src_ref=piece(way, delta, h), dst_ref=piece(way, delta + 1, h),
+            send_sem=a_send.at[way, delta, h], recv_sem=a_recv.at[way, delta, h],
+            device_id=(r, (c + 1 - 2 * way + n) % n, d), device_id_type=MESH,
+        )
+
+    def b_copy(source, half, way, k):
+        part = b_all.at[source, pl.ds(half * half_b, half_b)]
+        return pltpu.make_async_remote_copy(
+            src_ref=part, dst_ref=part,
+            send_sem=b_send.at[way, k], recv_sem=b_recv.at[source, half],
+            device_id=(across[way], c, d), device_id_type=MESH,
+        )
+
+    def ta_copy(s):
+        return pltpu.make_async_remote_copy(
+            src_ref=tab_a.at[c], dst_ref=tab_a.at[c],
+            send_sem=ta_send.at[s], recv_sem=ta_recv.at[c],
+            device_id=(r, z_peers[s], d), device_id_type=MESH,
+        )
+
+    def tb_copy(s):
+        return pltpu.make_async_remote_copy(
+            src_ref=tab_b.at[r], dst_ref=tab_b.at[r],
+            send_sem=tb_send.at[s], recv_sem=tb_recv.at[r],
+            device_id=(r_peers[s], c, d), device_id_type=MESH,
+        )
+
+    def wait_ta(source):
+        pltpu.make_async_remote_copy(
+            src_ref=tab_a.at[source], dst_ref=tab_a.at[source],
+            send_sem=ta_send.at[0], recv_sem=ta_recv.at[source],
+            device_id=(r, z_peers[0], d), device_id_type=MESH,
+        ).wait_recv()
+
+    def wait_tb(source):
+        pltpu.make_async_remote_copy(
+            src_ref=tab_b.at[source], dst_ref=tab_b.at[source],
+            send_sem=tb_send.at[0], recv_sem=tb_recv.at[source],
+            device_id=(r_peers[0], c, d), device_id_type=MESH,
+        ).wait_recv()
+
+    load_a.wait()
+    load_b.wait()
+    pl.semaphore_wait(barrier, 7)
+
+    for s in range(n - 1):
+        tb_copy(s).start()
+        ta_copy(s).start()
+    for h in range(NCH):
+        if h == 0:
+            b_copy(r, 0, 0, 0).start()
+            b_copy(r, 1, 1, 0).start()
+        if h == 1:
+            b_copy(r, 1, 0, 1).start()
+            b_copy(r, 0, 1, 1).start()
+
+        @pl.when(c < n - 1)
+        def _():
+            a_copy(0, 0, h).start()
+
+        @pl.when(c > 0)
+        def _():
+            a_copy(1, 0, h).start()
+
+    b_copy(across[0], 0, 1, 2).wait_recv()
+    b_copy(across[0], 0, 1, 2).start()
+    b_copy(across[1], 1, 0, 2).wait_recv()
+    b_copy(across[1], 1, 0, 2).start()
+
+    for s in range(n - 1):
+        wait_ta(z_peers[s])
+        wait_tb(r_peers[s])
+    fetch_a = pltpu.make_async_copy(tab_a, ind_a, ind_sem.at[0])
+    fetch_b = pltpu.make_async_copy(tab_b, ind_b, ind_sem.at[1])
+    fetch_a.start()
+    fetch_b.start()
+    fetch_a.wait()
+    fetch_b.wait()
+
+    def expand_b(source):
+        partner = (r + source - c + n) % n
+
+        def one(q, carry):
+            for j in range(CB):
+                block = b_all[partner, ind_b[partner, 0, q * CB + j]]
+                b_dense[j // 2, pl.ds(pl.multiple_of(q * side, side), side), pl.ds(j % 2 * side, side)] = block
+            return carry
+
+        lax.fori_loop(0, KB, one, 0)
+
+    def multiply(ref, source, h):
+        height = ref.shape[1]
+        at = pl.ds(h * height, height)
+        for i in range(RB):
+            for q in range(KB):
+                a_dense[pl.ds(i * height, height), pl.ds(q * side, side)] = ref[
+                    ind_a[source, 0, i * KB + q]
+                ]
+
+        def one(t, carry):
+            got = jnp.dot(
+                a_dense[pl.ds(0, RB * height)], b_dense[t], preferred_element_type=jnp.float32
+            )
+            for i in range(RB):
+                for j in range(2):
+                    total[i * CB + t * 2 + j, at] += got[
+                        i * height : (i + 1) * height, j * side : (j + 1) * side
+                    ]
+            return carry
+
+        lax.fori_loop(0, CB // 2, one, 0)
+
+    b_copy(across[0], 1, 0, 0).wait_recv()
+    b_copy(across[1], 0, 0, 0).wait_recv()
+    b_copy(corner, 0, 0, 0).wait_recv()
+    b_copy(corner, 1, 0, 0).wait_recv()
+
+    expand_b(c)
+    multiply(own, c, 0)
+
+    for delta in (1, 2):
+        behind = (c - delta, c + delta)
+        there = (behind[0] >= 0, behind[1] < n)
+        onward = (c < n - 1, c > 0)
+        for h in range(NCH):
+            for way in range(2):
+
+                @pl.when(there[way])
+                def _():
+                    a_copy(way, delta - 1, h).wait_recv()
+
+                    @pl.when(onward[way])
+                    def _():
+                        a_copy(way, delta, h).start()
+
+        if delta == 1:
+            for way in range(2):
+
+                @pl.when(there[way])
+                def _():
+                    expand_b(behind[way])
+                    multiply(held[way][1], behind[way], 0)
+
+        else:
+            source = jnp.where(there[0], behind[0], behind[1])
+            expand_b(source)
+            multiply(two, source, 0)
+
+    far = n - 1 - c
+    is_end = (c == 0) | (c == n - 1)
+
+    @pl.when(is_end)
+    def _():
+        expand_b(far)
+
+    def x_copy(h):
+        return pltpu.make_async_remote_copy(
+            src_ref=give.at[h], dst_ref=take.at[h],
+            send_sem=x_send.at[h], recv_sem=x_recv.at[h],
+            device_id=(r, c, 1 - d), device_id_type=MESH,
+        )
+
+    def finish(h):
+        at = pl.ds(h * rows, rows)
+        x_copy(h).wait_recv()
+        for t in range(mine):
+            out[t, at] = (total[c_idx[d * mine + t], at] + take[h, t]).astype(out.dtype)
+
+    for h in range(NCH):
+        at = pl.ds(h * rows, rows)
+        for way in range(2):
+
+            @pl.when(c == (n - 1) * (1 - way))
+            def _():
+                a_copy(way, n - 2, h).wait_recv()
+
+        @pl.when(is_end)
+        def _():
+            multiply(far_parts[h], far, h)
+
+        for t in range(mine):
+            give[h, t] = total[c_idx[(1 - d) * mine + t], at]
+        x_copy(h).start()
+        if h > 0:
+            finish(h - 1)
+    finish(NCH - 1)
+
+    for h in range(NCH):
+        x_copy(h).wait_send()
+        for way in range(2):
+            for delta in range(n - 1):
+                has = (c >= delta) & (c < n - 1) if way == 0 else (c + delta < n) & (c > 0)
+
+                @pl.when(has)
+                def _():
+                    a_copy(way, delta, h).wait_send()
+
+    for way in range(2):
+        for k in range(3):
+            b_copy(r, 0, way, k).wait_send()
+    for s in range(n - 1):
+        ta_copy(s).wait_send()
+        tb_copy(s).wait_send()
+
+
+def fast_body(left_block_slots, a_index, a_count, b_blocks, b_index, b_count, c_index):
+    slots_a, side = left_block_slots.shape[4], left_block_slots.shape[5]
+    slots_b = b_blocks.shape[4]
+    targets = c_index.shape[2]
+    mine = targets // 2
+    n = 4
+    bf, f32, i32 = jnp.bfloat16, jnp.float32, jnp.int32
+    rows = side // NCH
+    dma = pltpu.SemaphoreType.DMA
+    smem = pl.BlockSpec(memory_space=pltpu.SMEM)
+    hbm = pl.BlockSpec(memory_space=pl.ANY)
+    flops = 2 * RB * KB * CB * side**3 * n
+    out = pl.pallas_call(
+        fast_kernel,
+        out_shape=jax.ShapeDtypeStruct((mine, side, side), bf),
+        in_specs=[hbm, hbm, smem, smem, smem, smem, smem],
+        out_specs=pl.BlockSpec(memory_space=pltpu.VMEM),
+        scratch_shapes=[
+            pltpu.VMEM((slots_a + 1, side, side), bf),
+            pltpu.VMEM((slots_a + 1, side, side), bf),
+            pltpu.VMEM((slots_a + 1, side, side), bf),
+            pltpu.VMEM((slots_a + 1, side, side), bf),
+            tuple(pltpu.VMEM((slots_a + 1, rows, side), bf) for h in range(NCH)),
+            pltpu.VMEM((n, slots_b + 1, side, side), bf),
+            pltpu.VMEM((n, 8, 128), i32),
+            pltpu.VMEM((n, 8, 128), i32),
+            pltpu.SMEM((n, 8, 128), i32),
+            pltpu.SMEM((n, 8, 128), i32),
+            pltpu.VMEM((CB // 2, KB * side, 2 * side), bf),
+            pltpu.VMEM((RB * side, KB * side), bf),
+            pltpu.VMEM((RB * CB, side, side), f32),
+            pltpu.VMEM((NCH, mine, rows, side), f32),
+            pltpu.VMEM((NCH, mine, rows, side), f32),
+            dma((2,)),
+            dma((2,)),
+            dma((2, n - 1, NCH)),
+            dma((2, n - 1, NCH)),
+            dma((2, 3)),
+            dma((n, 2)),
+            dma((n - 1,)),
+            dma((n,)),
+            dma((n - 1,)),
+            dma((n,)),
+            dma((NCH,)),
+            dma((NCH,)),
+        ],
+        compiler_params=pltpu.CompilerParams(
+            collective_id=0, has_side_effects=True, vmem_limit_bytes=32 * 1024 * 1024
+        ),
+        cost_estimate=pl.CostEstimate(flops=flops, bytes_accessed=4 << 20, transcendentals=0),
+    )(
+        left_block_slots[0, 0, 0, 0],
+        b_blocks[0, 0, 0, 0],
+        a_index[0, 0, 0, 0],
+        a_count[0, 0, 0],
+        b_index[0, 0, 0, 0],
+        b_count[0, 0, 0],
+        c_index[0, 0],
+    )
+    return out[None, None]
+
+
 def solution(mesh):
     placed = (
         P("row", "col", "depth", None, None, None, None),
@@ -135,8 +471,9 @@
         P("row", "col", "depth", None),
         P("row", "col", None),
     )
+    square = (mesh.shape["row"], mesh.shape["col"], mesh.shape["depth"]) == (4, 4, 2)
     return jax.shard_map(
-        body,
+        fast_body if square else body,
         mesh=mesh,
         in_specs=placed,
         out_specs=P("row", "col", "depth", None, None),

time: 170 us -> 49.2 us (0.29)
  matrix products: 46.3 us -> 0 us
  starting transfers between devices: 45.2 us -> 0 us
  Pallas kernels: 0 us -> 44.3 us
  local copies, waits for them, and re-layouts: 41.9 us -> 3.4 us
  between operations: 14.7 us -> 1.33 us
  waiting for transfers between devices: 12.6 us -> 0 us
  loops' own time: 4.2 us -> 0 us
  other arithmetic: 3.55 us -> 0 us
    dot_general x8 -> x0, matrix products: 46.3 us -> none  [the longest x4 28.4 us: contribute(): jnp.einsum('oxmn,oxnw->omw', left_strip, right_strip, preferred_element_t...]
    ppermute x18 -> x0, starting transfers between devices: 45.2 us -> none  [from_behind(): return lax.ppermute(value, axis, pairs)]
    pallas_call x0 -> x1, Pallas kernels: none -> 44.3 us  [fast_body(): pl.pallas_call(fast_kernel, out_shape=jax.ShapeDtypeStruct((mine, side, s...]
    reshape x4 -> x0, local copies, waits for them, and re-layouts: 37.7 us -> none  [select_blocks(): return chosen.reshape(wanted.shape + (side, side))]
    reduce_scatter x1 -> x0, waiting for transfers between devices: 8.52 us -> none  [body(): lax.psum_scatter(product_total, 'depth', scatter_dimension=0, tiled=True)]
    another operation x1 -> x0, loops' own time: 4.2 us -> none  [run_round(): lax.fori_loop(0, length - 1, inner, (a_now, b_now, product_total))]
    ppermute x18 -> x0, waiting for transfers between devices: 4.06 us -> none  [from_behind(): return lax.ppermute(value, axis, pairs)]
    broadcast_in_dim x1 -> x0, other arithmetic: 1.95 us -> none  [body(): return shares.astype(jnp.bfloat16)[None, None]]
  transfers between devices with their start and end apart: 19 -> 0, of which waited for: 4 -> 0; matrix products, arithmetic and copies ran while one was open for 38% -> 0% of each run, Pallas kernels for 0% -> 0%
where the time goes in v1:
time: 49.2 us; the launch traced here: 49 us
  Pallas kernels  44.3 us (90%)
  local copies, waits for them, and re-layouts  3.4 us (7%)
  between operations  1.33 us (3%)
    pallas_call x1, Pallas kernels, fast_body(): pl.pallas_call(fast_kernel, out_shape=jax.ShapeDtypeStruct((mine, side, s...  44.3 us
    unnamed x11, local copies, waits for them, and re-layouts  3.4 us

profile of v1, /device:TPU:0, one launch (start us, length us, event | category | flops | bytes accessed | tf_op | source)
XLA Modules:
  0.0 49.0 jit_solution(10879846841920401853)
XLA Ops:
  1.3 0.0 copy-start.2
  1.3 0.0 copy-start.3
  1.3 0.0 copy-start.4
  1.3 0.6 %copy-done.2 = s32[1,1,1,1,16]{4,3,2,1,0:T(1,128)S(1)} copy-done((s32[1,1,1,1,16]{4,3,2,1,0:T(1,128)S(1)}, s32[1,1,1,1,16]{4,3,2,1,0:T(1,128)}, u32[]{:S(2)}) %copy-start.2) | copy-done | bytes 88
  2.0 0.0 copy-done.3
  2.0 0.0 copy-done.4
  2.0 0.0 copy-start
  2.0 1.0 %copy-done = bf16[1,1,1,1,16,128,128]{6,5,4,3,2,1,0:T(8,128)(2,1)S(1)} copy-done((bf16[1,1,1,1,16,128,128]{6,5,4,3,2,1,0:T(8,128)(2,1)S(1)}, bf16[1,1,1,1,16,128,128]{6,5,4,3,2,1,0:T(8,128)(2,1)}, u32[]{:S(2)}) %copy-start) | copy-done | bytes 524312
  3.0 0.0 copy-start.1
  3.0 0.9 %copy-done.1 = bf16[1,1,1,1,8,128,128]{6,5,4,3,2,1,0:T(8,128)(2,1)S(1)} copy-done((bf16[1,1,1,1,8,128,128]{6,5,4,3,2,1,0:T(8,128)(2,1)S(1)}, bf16[1,1,1,1,8,128,128]{6,5,4,3,2,1,0:T(8,128)(2,1)}, u32[]{:S(2)}) %copy-start.1) | copy-done | bytes 262168
  4.0 44.3 %shard_map.73 = bf16[12,128,128]{2,1,0:T(8,128)(2,1)S(1)} custom-call(bf16[16,128,128]{2,1,0:T(8,128)(2,1)S(1)} %bitcast.11, bf16[8,128,128]{2,1,0:T(8,128)(2,1)S(1)} %bitcast.12, s32[16]{0:T(128)S(1)} %bitcast.13, s32[1]{0:T(128)} %bitcast.8.a_cnt, s32[8]{0:T(128)S(1)} %bitcast.14, s32[1]{0:T(128)} %bitcast.9.b_cnt, s32[24]{0:T(128)S(1)} %bitcast.15), custom_call_target="tpu_custom_call" | custom-call | flops 4294967296 | bytes 4194304 | tf_op jit(solution)/shard_map/pallas_call | solution.py:414
  48.3 0.7 %copy.11 = bf16[1,1,12,128,128]{4,3,2,1,0:T(8,128)(2,1)} copy(bf16[1,1,12,128,128]{4,3,2,1,0:T(8,128)(2,1)S(1)} %bitcast.10) | data formatting | bytes 786432
Async XLA Ops:
  1.3 0.7 %copy-start.2 = (s32[1,1,1,1,16]{4,3,2,1,0:T(1,128)S(1)}, s32[1,1,1,1,16]{4,3,2,1,0:T(1,128)}, u32[]{:S(2)}) copy-start(s32[1,1,1,1,16]{4,3,2,1,0:T(1,128)} %param.8) | copy-start | bytes 196
  1.3 0.7 %copy-start.3 = (s32[1,1,1,1,8]{4,3,2,1,0:T(1,128)S(1)}, s32[1,1,1,1,8]{4,3,2,1,0:T(1,128)}, u32[]{:S(2)}) copy-start(s32[1,1,1,1,8]{4,3,2,1,0:T(1,128)} %param.11) | copy-start | bytes 100
  1.3 0.7 %copy-start.4 = (s32[1,1,24]{2,1,0:T(1,128)S(1)}, s32[1,1,24]{2,1,0:T(1,128)}, u32[]{:S(2)}) copy-start(s32[1,1,24]{2,1,0:T(1,128)} %param.13) | copy-start | bytes 292
  2.0 1.0 %copy-start = (bf16[1,1,1,1,16,128,128]{6,5,4,3,2,1,0:T(8,128)(2,1)S(1)}, bf16[1,1,1,1,16,128,128]{6,5,4,3,2,1,0:T(8,128)(2,1)}, u32[]{:S(2)}) copy-start(bf16[1,1,1,1,16,128,128]{6,5,4,3,2,1,0:T(8,128)(2,1)} %param.7) | copy-start | bytes 1572868
  3.0 0.9 %copy-start.1 = (bf16[1,1,1,1,8,128,128]{6,5,4,3,2,1,0:T(8,128)(2,1)S(1)}, bf16[1,1,1,1,8,128,128]{6,5,4,3,2,1,0:T(8,128)(2,1)}, u32[]{:S(2)}) copy-start(bf16[1,1,1,1,8,128,128]{6,5,4,3,2,1,0:T(8,128)(2,1)} %param.10) | copy-start | bytes 786436

commit v2 on v0

--- a/solution.py
+++ b/solution.py
@@ -1,10 +1,15 @@
 import jax
 import jax.numpy as jnp
 from jax import lax
+from jax.experimental import pallas as pl
+from jax.experimental.pallas import tpu as pltpu
 from jax.sharding import PartitionSpec as P
 
+RB = 4
 KB = 8
 CB = 8
+NCH = 4
+MESH = pl.DeviceIdType.MESH
 
 
 def from_behind(value, axis, steps):
@@ -125,6 +130,394 @@
     return shares.astype(jnp.bfloat16)[None, None]
 
 
+def fast_kernel(
+    a_hbm, b_hbm, a_idx, a_cnt, b_idx, b_cnt, c_idx, out,
+    own, near, other, far, b_mine, b_mate, tab_a, tab_b, tab_e, ind_a, ind_b, ind_e,
+    b_dense, a_dense, total, give, take, ready, result,
+    local_sem, ind_sem, a_send, a_recv, b_send, b_recv, e_send,
+    ta_send, ta_recv, tb_send, tb_recv, te_recv, x_send, x_recv, o_send, o_recv,
+):
+    r = lax.axis_index("row")
+    c = lax.axis_index("col")
+    d = lax.axis_index("depth")
+    n = 4
+    slots_a, side = a_hbm.shape[0], a_hbm.shape[1]
+    slots_b = b_hbm.shape[0]
+    half_b = slots_b // 2
+    rows = side // NCH
+    mine = out.shape[0]
+    x, y = r % 2, r // 2
+    across = (y * 2 + (1 - x), (1 - y) * 2 + x)
+    corner = (1 - y) * 2 + (1 - x)
+    mate = c + 1 - 2 * (c % 2)
+    inner = (c == 1) | (c == 2)
+    is_end = (c == 0) | (c == 3)
+    opposite = 3 - c
+    far_end = 3 - mate
+
+    barrier = pltpu.get_barrier_semaphore()
+    z_peers = [(c + s) % n for s in range(1, n)]
+    r_peers = [(r + s) % n for s in range(1, n)]
+    for z in z_peers:
+        pl.semaphore_signal(barrier, inc=1, device_id=(r, z, d), device_id_type=MESH)
+    for q in r_peers:
+        pl.semaphore_signal(barrier, inc=1, device_id=(q, c, d), device_id_type=MESH)
+        pl.semaphore_signal(barrier, inc=1, device_id=(q, mate, d), device_id_type=MESH)
+    pl.semaphore_signal(barrier, inc=1, device_id=(r, c, 1 - d), device_id_type=MESH)
+
+    load_a = pltpu.make_async_copy(a_hbm, own.at[pl.ds(0, slots_a)], local_sem.at[0])
+    load_b = pltpu.make_async_copy(b_hbm, b_mine.at[r, pl.ds(0, slots_b)], local_sem.at[1])
+    load_a.start()
+    load_b.start()
+
+    lane = lax.broadcasted_iota(jnp.int32, (8, 128), 1)
+    line = lax.broadcasted_iota(jnp.int32, (8, 128), 0)
+    inv_a = jnp.full((8, 128), slots_a, jnp.int32)
+    for s in range(slots_a):
+        inv_a = jnp.where((lane == a_idx[s]) & (s < a_cnt[0]), s, inv_a)
+    goals = jnp.zeros((8, 128), jnp.int32)
+    for t in range(2 * mine):
+        goals = jnp.where(lane == t, c_idx[t], goals)
+    inv_b = jnp.full((8, 128), slots_b, jnp.int32)
+    for s in range(slots_b):
+        inv_b = jnp.where((lane == b_idx[s]) & (s < b_cnt[0]), s, inv_b)
+    tab_a[c] = jnp.where(line == 1, goals, inv_a)
+    tab_b[r] = inv_b
+
+    def a_copy(kind, h):
+        at = (pl.ds(0, slots_a), pl.ds(h * rows, rows))
+        if kind == 0:
+            source, target, to = own.at[at], near.at[at], mate
+        elif kind == 1:
+            source, target, to = own.at[at], other.at[at], opposite
+        else:
+            source, target, to = near.at[at], far[h].at[pl.ds(0, slots_a)], opposite
+        return pltpu.make_async_remote_copy(
+            src_ref=source, dst_ref=target,
+            send_sem=a_send.at[kind, h], recv_sem=a_recv.at[kind, h],
+            device_id=(r, to, d), device_id_type=MESH,
+        )
+
+    columns = (b_mine, b_mate)
+
+    def b_copy(column, source, half, way, k):
+        part = columns[column].at[source, pl.ds(half * half_b, half_b)]
+        return pltpu.make_async_remote_copy(
+            src_ref=part, dst_ref=part,
+            send_sem=b_send.at[column, way, k], recv_sem=b_recv.at[column, source, half],
+            device_id=(across[way], c, d), device_id_type=MESH,
+        )
+
+    def e_copy(half):
+        at = pl.ds(half * half_b, half_b)
+        return pltpu.make_async_remote_copy(
+            src_ref=b_mine.at[r, at], dst_ref=b_mate.at[r, at],
+            send_sem=e_send.at[half], recv_sem=b_recv.at[1, r, half],
+            device_id=(r, mate, d), device_id_type=MESH,
+        )
+
+    def ta_copy(source, to, k):
+        return pltpu.make_async_remote_copy(
+            src_ref=tab_a.at[source], dst_ref=tab_a.at[source],
+            send_sem=ta_send.at[k], recv_sem=ta_recv.at[source],
+            device_id=(r, to, d), device_id_type=MESH,
+        )
+
+    def tb_copy(source, to, k):
+        return pltpu.make_async_remote_copy(
+            src_ref=tab_b.at[source], dst_ref=tab_b.at[source],
+            send_sem=tb_send.at[k], recv_sem=tb_recv.at[source],
+            device_id=(to, c, d), device_id_type=MESH,
+        )
+
+    def te_copy(source, to, k):
+        return pltpu.make_async_remote_copy(
+            src_ref=tab_b.at[source], dst_ref=tab_e.at[source],
+            send_sem=tb_send.at[k], recv_sem=te_recv.at[source],
+            device_id=(to, mate, d), device_id_type=MESH,
+        )
+
+    def x_copy(column, h):
+        return pltpu.make_async_remote_copy(
+            src_ref=give.at[column, h], dst_ref=take.at[column, h],
+            send_sem=x_send.at[column, h], recv_sem=x_recv.at[column, h],
+            device_id=(r, c, 1 - d), device_id_type=MESH,
+        )
+
+    def o_copy(h):
+        return pltpu.make_async_remote_copy(
+            src_ref=ready.at[h], dst_ref=result.at[h],
+            send_sem=o_send.at[h], recv_sem=o_recv.at[h],
+            device_id=(r, mate, d), device_id_type=MESH,
+        )
+
+    load_a.wait()
+    load_b.wait()
+    pl.semaphore_wait(barrier, 10)
+
+    @pl.when(is_end)
+    def _():
+        e_copy(0).start()
+        e_copy(1).start()
+        for q in range(n):
+            te_copy(r, (r + q) % n, q).start()
+        ta_copy(c, mate, 0).start()
+        ta_copy(c, 3 - mate, 1).start()
+        for h in range(NCH):
+            a_copy(0, h).start()
+        for h in range(NCH):
+            o_copy(h).wait_recv()
+            for t in range(mine):
+                out[t, pl.ds(h * rows, rows)] = result[h, t]
+        for h in range(NCH):
+            a_copy(0, h).wait_send()
+        for half in range(2):
+            e_copy(half).wait_send()
+        for q in range(n):
+            te_copy(r, r, q).wait_send()
+        for k in range(2):
+            ta_copy(c, mate, k).wait_send()
+
+    def expand_b(column, source):
+        place = c if column == 0 else mate
+        partner = (r + source - place + n) % n
+        held, index = columns[column], (ind_b, ind_e)[column]
+
+        def one(q, carry):
+            for j in range(CB):
+                b_dense[
+                    column, j // 2, pl.ds(pl.multiple_of(q * side, side), side), pl.ds(j % 2 * side, side)
+                ] = held[partner, index[partner, 0, q * CB + j]]
+            return carry
+
+        lax.fori_loop(0, KB, one, 0)
+
+    def expand_a(k, ref, source):
+        height = ref.shape[1]
+        for i in range(RB):
+            for q in range(KB):
+                a_dense[k, pl.ds(i * height, height), pl.ds(q * side, side)] = ref[
+                    ind_a[source, 0, i * KB + q]
+                ]
+
+    def multiply(column, k, height, h):
+        at = pl.ds(h * height, height)
+
+        def one(t, carry):
+            got = jnp.dot(
+                a_dense[k, pl.ds(0, RB * height)], b_dense[column, t],
+                preferred_element_type=jnp.float32,
+            )
+            for i in range(RB):
+                for j in range(2):
+                    total[column, i * CB + t * 2 + j, at] += got[
+                        i * height : (i + 1) * height, j * side : (j + 1) * side
+                    ]
+            return carry
+
+        lax.fori_loop(0, CB // 2, one, 0)
+
+    def b_first(column):
+        b_copy(column, r, 0, 0, 0).start()
+        b_copy(column, r, 1, 1, 0).start()
+        b_copy(column, r, 1, 0, 1).start()
+        b_copy(column, r, 0, 1, 1).start()
+
+    def b_onward(column):
+        b_copy(column, across[0], 0, 1, 2).wait_recv()
+        b_copy(column, across[0], 0, 1, 2).start()
+        b_copy(column, across[1], 1, 0, 2).wait_recv()
+        b_copy(column, across[1], 1, 0, 2).start()
+
+    def b_rest(column):
+        b_copy(column, across[0], 1, 0, 0).wait_recv()
+        b_copy(column, across[1], 0, 0, 0).wait_recv()
+        b_copy(column, corner, 0, 0, 0).wait_recv()
+        b_copy(column, corner, 1, 0, 0).wait_recv()
+
+    def relay(h):
+        a_copy(0, h).wait_recv()
+        a_copy(2, h).start()
+
+    def finish(h):
+        at = pl.ds(h * rows, rows)
+        x_copy(1, h).wait_recv()
+        for t in range(mine):
+            ready[h, t] = (total[1, ind_a[mate, 1, d * mine + t], at] + take[1, h, t]).astype(out.dtype)
+        o_copy(h).start()
+        x_copy(0, h).wait_recv()
+        for t in range(mine):
+            out[t, at] = (total[0, c_idx[d * mine + t], at] + take[0, h, t]).astype(out.dtype)
+
+    @pl.when(inner)
+    def _():
+        for s in range(n - 1):
+            tb_copy(r, r_peers[s], s).start()
+        ta_copy(c, opposite, 0).start()
+        b_first(0)
+        for h in range(NCH):
+            a_copy(1, h).start()
+
+        for p in range(n):
+            b_mine[p, slots_b] = jnp.zeros((side, side), b_mine.dtype)
+            b_mate[p, slots_b] = jnp.zeros((side, side), b_mate.dtype)
+        for ref in (own, near, other):
+            ref[slots_a] = jnp.zeros((side, side), ref.dtype)
+        for ref in far:
+            ref[slots_a] = jnp.zeros((rows, side), ref.dtype)
+
+        def zero(t, carry):
+            total[0, t] = jnp.zeros((side, side), jnp.float32)
+            total[1, t] = jnp.zeros((side, side), jnp.float32)
+            return carry
+
+        lax.fori_loop(0, RB * CB, zero, 0)
+
+        for s in range(n - 1):
+            ta_copy(z_peers[s], opposite, 0).wait_recv()
+            tb_copy(r_peers[s], r, 0).wait_recv()
+        for q in range(n):
+            te_copy(q, r, 0).wait_recv()
+        fetches = [
+            pltpu.make_async_copy(tab, ind, ind_sem.at[k])
+            for k, (tab, ind) in enumerate(((tab_a, ind_a), (tab_b, ind_b), (tab_e, ind_e)))
+        ]
+        for fetch in fetches:
+            fetch.start()
+        for fetch in fetches:
+            fetch.wait()
+        expand_a(0, own, c)
+
+        b_onward(0)
+        e_copy(0).wait_recv()
+        e_copy(1).wait_recv()
+        b_first(1)
+        relay(0)
+        b_rest(0)
+        expand_b(0, c)
+        multiply(0, 0, side, 0)
+        relay(1)
+        for h in range(NCH):
+            a_copy(1, h).wait_recv()
+        expand_a(1, other, opposite)
+        expand_b(0, opposite)
+        multiply(0, 1, side, 0)
+        b_onward(1)
+        for h in range(2, NCH):
+            relay(h)
+        expand_a(2, near, mate)
+        expand_b(0, mate)
+        multiply(0, 2, side, 0)
+        expand_b(0, far_end)
+        b_rest(1)
+        for k, source in enumerate((c, opposite, mate)):
+            expand_b(1, source)
+            multiply(1, k, side, 0)
+        expand_b(1, far_end)
+
+        for h in range(NCH):
+            at = pl.ds(h * rows, rows)
+            a_copy(2, h).wait_recv()
+            expand_a(0, far[h], far_end)
+            multiply(1, 0, rows, h)
+            for t in range(mine):
+                give[1, h, t] = total[1, ind_a[mate, 1, (1 - d) * mine + t], at]
+            x_copy(1, h).start()
+            multiply(0, 0, rows, h)
+            for t in range(mine):
+                give[0, h, t] = total[0, c_idx[(1 - d) * mine + t], at]
+            x_copy(0, h).start()
+            if h > 0 and h < NCH - 1:
+                finish(h - 1)
+            elif h == NCH - 1:
+                finish(h - 1)
+                finish(h)
+
+        for h in range(NCH):
+            for column in range(2):
+                x_copy(column, h).wait_send()
+            a_copy(1, h).wait_send()
+            a_copy(2, h).wait_send()
+            o_copy(h).wait_send()
+        for column in range(2):
+            for way in range(2):
+                for k in range(3):
+                    b_copy(column, r, 0, way, k).wait_send()
+        for s in range(n - 1):
+            tb_copy(r, r, s).wait_send()
+        ta_copy(c, opposite, 0).wait_send()
+
+
+def fast_body(left_block_slots, a_index, a_count, b_blocks, b_index, b_count, c_index):
+    slots_a, side = left_block_slots.shape[4], left_block_slots.shape[5]
+    slots_b = b_blocks.shape[4]
+    targets = c_index.shape[2]
+    mine = targets // 2
+    n = 4
+    bf, f32, i32 = jnp.bfloat16, jnp.float32, jnp.int32
+    rows = side // NCH
+    dma = pltpu.SemaphoreType.DMA
+    smem = pl.BlockSpec(memory_space=pltpu.SMEM)
+    hbm = pl.BlockSpec(memory_space=pl.ANY)
+    flops = 2 * RB * KB * CB * side**3 * n
+    out = pl.pallas_call(
+        fast_kernel,
+        out_shape=jax.ShapeDtypeStruct((mine, side, side), bf),
+        in_specs=[hbm, hbm, smem, smem, smem, smem, smem],
+        out_specs=pl.BlockSpec(memory_space=pltpu.VMEM),
+        scratch_shapes=[
+            pltpu.VMEM((slots_a + 1, side, side), bf),
+            pltpu.VMEM((slots_a + 1, side, side), bf),
+            pltpu.VMEM((slots_a + 1, side, side), bf),
+            tuple(pltpu.VMEM((slots_a + 1, rows, side), bf) for h in range(NCH)),
+            pltpu.VMEM((n, slots_b + 1, side, side), bf),
+            pltpu.VMEM((n, slots_b + 1, side, side), bf),
+            pltpu.VMEM((n, 8, 128), i32),
+            pltpu.VMEM((n, 8, 128), i32),
+            pltpu.VMEM((n, 8, 128), i32),
+            pltpu.SMEM((n, 8, 128), i32),
+            pltpu.SMEM((n, 8, 128), i32),
+            pltpu.SMEM((n, 8, 128), i32),
+            pltpu.VMEM((2, CB // 2, KB * side, 2 * side), bf),
+            pltpu.VMEM((3, RB * side, KB * side), bf),
+            pltpu.VMEM((2, RB * CB, side, side), f32),
+            pltpu.VMEM((2, NCH, mine, rows, side), f32),
+            pltpu.VMEM((2, NCH, mine, rows, side), f32),
+            pltpu.VMEM((NCH, mine, rows, side), bf),
+            pltpu.VMEM((NCH, mine, rows, side), bf),
+            dma((2,)),
+            dma((3,)),
+            dma((3, NCH)),
+            dma((3, NCH)),
+            dma((2, 2, 3)),
+            dma((2, n, 2)),
+            dma((2,)),
+            dma((2,)),
+            dma((n,)),
+            dma((n,)),
+            dma((n,)),
+            dma((n,)),
+            dma((2, NCH)),
+            dma((2, NCH)),
+            dma((NCH,)),
+            dma((NCH,)),
+        ],
+        compiler_params=pltpu.CompilerParams(
+            collective_id=0, has_side_effects=True, vmem_limit_bytes=40 * 1024 * 1024
+        ),
+        cost_estimate=pl.CostEstimate(flops=flops, bytes_accessed=4 << 20, transcendentals=0),
+    )(
+        left_block_slots[0, 0, 0, 0],
+        b_blocks[0, 0, 0, 0],
+        a_index[0, 0, 0, 0],
+        a_count[0, 0, 0],
+        b_index[0, 0, 0, 0],
+        b_count[0, 0, 0],
+        c_index[0, 0],
+    )
+    return out[None, None]
+
+
 def solution(mesh):
     placed = (
         P("row", "col", "depth", None, None, None, None),
@@ -135,8 +528,9 @@
         P("row", "col", "depth", None),
         P("row", "col", None),
     )
+    square = (mesh.shape["row"], mesh.shape["col"], mesh.shape["depth"]) == (4, 4, 2)
     return jax.shard_map(
-        body,
+        fast_body if square else body,
         mesh=mesh,
         in_specs=placed,
         out_specs=P("row", "col", "depth", None, None),

time: 170 us -> 58.8 us (0.35)
  Pallas kernels: 0 us -> 53.9 us
  matrix products: 46.3 us -> 0 us
  starting transfers between devices: 45.2 us -> 0 us
  local copies, waits for them, and re-layouts: 41.9 us -> 3.4 us
  between operations: 14.7 us -> 1.33 us
  waiting for transfers between devices: 12.6 us -> 0 us
  loops' own time: 4.2 us -> 0 us
  other arithmetic: 3.55 us -> 0 us
    pallas_call x0 -> x1, Pallas kernels: none -> 53.9 us  [fast_body(): pl.pallas_call(fast_kernel, out_shape=jax.ShapeDtypeStruct((mine, side, s...]
    dot_general x8 -> x0, matrix products: 46.3 us -> none  [the longest x4 28.4 us: contribute(): jnp.einsum('oxmn,oxnw->omw', left_strip, right_strip, preferred_element_t...]
    ppermute x18 -> x0, starting transfers between devices: 45.2 us -> none  [from_behind(): return lax.ppermute(value, axis, pairs)]
    reshape x4 -> x0, local copies, waits for them, and re-layouts: 37.7 us -> none  [select_blocks(): return chosen.reshape(wanted.shape + (side, side))]
    reduce_scatter x1 -> x0, waiting for transfers between devices: 8.52 us -> none  [body(): lax.psum_scatter(product_total, 'depth', scatter_dimension=0, tiled=True)]
    another operation x1 -> x0, loops' own time: 4.2 us -> none  [run_round(): lax.fori_loop(0, length - 1, inner, (a_now, b_now, product_total))]
    ppermute x18 -> x0, waiting for transfers between devices: 4.06 us -> none  [from_behind(): return lax.ppermute(value, axis, pairs)]
    broadcast_in_dim x1 -> x0, other arithmetic: 1.95 us -> none  [body(): return shares.astype(jnp.bfloat16)[None, None]]
  transfers between devices with their start and end apart: 19 -> 0, of which waited for: 4 -> 0; matrix products, arithmetic and copies ran while one was open for 38% -> 0% of each run, Pallas kernels for 0% -> 0%
where the time goes in v2:
time: 58.8 us; the launch traced here: 58.6 us
  Pallas kernels  53.9 us (92%)
  local copies, waits for them, and re-layouts  3.4 us (6%)
  between operations  1.33 us (2%)
    pallas_call x1, Pallas kernels, fast_body(): pl.pallas_call(fast_kernel, out_shape=jax.ShapeDtypeStruct((mine, side, s...  53.9 us
    unnamed x11, local copies, waits for them, and re-layouts  3.4 us

profile of v2, /device:TPU:0, one launch (start us, length us, event | category | flops | bytes accessed | tf_op | source)
XLA Modules:
  0.0 58.6 jit_solution(9107401175624265323)
XLA Ops:
  1.3 0.0 copy-start.2
  1.3 0.0 copy-start.3
  1.3 0.0 copy-start.4
  1.3 0.6 %copy-done.2 = s32[1,1,1,1,16]{4,3,2,1,0:T(1,128)S(1)} copy-done((s32[1,1,1,1,16]{4,3,2,1,0:T(1,128)S(1)}, s32[1,1,1,1,16]{4,3,2,1,0:T(1,128)}, u32[]{:S(2)}) %copy-start.2) | copy-done | bytes 88
  2.0 0.0 copy-done.3
  2.0 0.0 copy-done.4
  2.0 0.0 copy-start
  2.0 1.0 %copy-done = bf16[1,1,1,1,16,128,128]{6,5,4,3,2,1,0:T(8,128)(2,1)S(1)} copy-done((bf16[1,1,1,1,16,128,128]{6,5,4,3,2,1,0:T(8,128)(2,1)S(1)}, bf16[1,1,1,1,16,128,128]{6,5,4,3,2,1,0:T(8,128)(2,1)}, u32[]{:S(2)}) %copy-start) | copy-done | bytes 524312
  3.0 0.0 copy-start.1
  3.0 0.9 %copy-done.1 = bf16[1,1,1,1,8,128,128]{6,5,4,3,2,1,0:T(8,128)(2,1)S(1)} copy-done((bf16[1,1,1,1,8,128,128]{6,5,4,3,2,1,0:T(8,128)(2,1)S(1)}, bf16[1,1,1,1,8,128,128]{6,5,4,3,2,1,0:T(8,128)(2,1)}, u32[]{:S(2)}) %copy-start.1) | copy-done | bytes 262168
  4.0 53.9 %shard_map.73 = bf16[12,128,128]{2,1,0:T(8,128)(2,1)S(1)} custom-call(bf16[16,128,128]{2,1,0:T(8,128)(2,1)S(1)} %bitcast.11, bf16[8,128,128]{2,1,0:T(8,128)(2,1)S(1)} %bitcast.12, s32[16]{0:T(128)S(1)} %bitcast.13, s32[1]{0:T(128)} %bitcast.8.a_cnt, s32[8]{0:T(128)S(1)} %bitcast.14, s32[1]{0:T(128)} %bitcast.9.b_cnt, s32[24]{0:T(128)S(1)} %bitcast.15), custom_call_target="tpu_custom_call" | custom-call | flops 4294967296 | bytes 4194304 | tf_op jit(solution)/shard_map/pallas_call | solution.py:463
  57.9 0.7 %copy.11 = bf16[1,1,12,128,128]{4,3,2,1,0:T(8,128)(2,1)} copy(bf16[1,1,12,128,128]{4,3,2,1,0:T(8,128)(2,1)S(1)} %bitcast.10) | data formatting | bytes 786432
Async XLA Ops:
  1.3 0.7 %copy-start.2 = (s32[1,1,1,1,16]{4,3,2,1,0:T(1,128)S(1)}, s32[1,1,1,1,16]{4,3,2,1,0:T(1,128)}, u32[]{:S(2)}) copy-start(s32[1,1,1,1,16]{4,3,2,1,0:T(1,128)} %param.8) | copy-start | bytes 196
  1.3 0.7 %copy-start.3 = (s32[1,1,1,1,8]{4,3,2,1,0:T(1,128)S(1)}, s32[1,1,1,1,8]{4,3,2,1,0:T(1,128)}, u32[]{:S(2)}) copy-start(s32[1,1,1,1,8]{4,3,2,1,0:T(1,128)} %param.11) | copy-start | bytes 100
  1.3 0.7 %copy-start.4 = (s32[1,1,24]{2,1,0:T(1,128)S(1)}, s32[1,1,24]{2,1,0:T(1,128)}, u32[]{:S(2)}) copy-start(s32[1,1,24]{2,1,0:T(1,128)} %param.13) | copy-start | bytes 292
  2.0 1.0 %copy-start = (bf16[1,1,1,1,16,128,128]{6,5,4,3,2,1,0:T(8,128)(2,1)S(1)}, bf16[1,1,1,1,16,128,128]{6,5,4,3,2,1,0:T(8,128)(2,1)}, u32[]{:S(2)}) copy-start(bf16[1,1,1,1,16,128,128]{6,5,4,3,2,1,0:T(8,128)(2,1)} %param.7) | copy-start | bytes 1572868
  3.0 0.9 %copy-start.1 = (bf16[1,1,1,1,8,128,128]{6,5,4,3,2,1,0:T(8,128)(2,1)S(1)}, bf16[1,1,1,1,8,128,128]{6,5,4,3,2,1,0:T(8,128)(2,1)}, u32[]{:S(2)}) copy-start(bf16[1,1,1,1,8,128,128]{6,5,4,3,2,1,0:T(8,128)(2,1)} %param.10) | copy-start | bytes 786436

commit v3 on v1

--- a/solution.py
+++ b/solution.py
@@ -306,14 +306,6 @@
 
         lax.fori_loop(0, CB // 2, one, 0)
 
-    b_copy(across[0], 1, 0, 0).wait_recv()
-    b_copy(across[1], 0, 0, 0).wait_recv()
-    b_copy(corner, 0, 0, 0).wait_recv()
-    b_copy(corner, 1, 0, 0).wait_recv()
-
-    expand_b(c)
-    multiply(own, c, 0)
-
     for delta in (1, 2):
         behind = (c - delta, c + delta)
         there = (behind[0] >= 0, behind[1] < n)
@@ -330,6 +322,12 @@
                         a_copy(way, delta, h).start()
 
         if delta == 1:
+            b_copy(across[0], 1, 0, 0).wait_recv()
+            b_copy(across[1], 0, 0, 0).wait_recv()
+            b_copy(corner, 0, 0, 0).wait_recv()
+            b_copy(corner, 1, 0, 0).wait_recv()
+            expand_b(c)
+            multiply(own, c, 0)
             for way in range(2):
 
                 @pl.when(there[way])
@@ -446,7 +444,7 @@
             dma((NCH,)),
         ],
         compiler_params=pltpu.CompilerParams(
-            collective_id=0, has_side_effects=True, vmem_limit_bytes=32 * 1024 * 1024
+            collective_id=0, has_side_effects=True, vmem_limit_bytes=60 * 1024 * 1024
         ),
         cost_estimate=pl.CostEstimate(flops=flops, bytes_accessed=4 << 20, transcendentals=0),
     )(

time: 49.2 us -> 47.6 us (0.967)
  local copies, waits for them, and re-layouts: 3.4 us -> 1.77 us
    unnamed x11 -> x1, local copies, waits for them, and re-layouts: 3.4 us -> 1.77 us
where the time goes in v3:
time: 47.6 us; the launch traced here: 47.5 us
  Pallas kernels  44.4 us (93%)
  local copies, waits for them, and re-layouts  1.77 us (4%)
  between operations  1.3 us (3%)
    pallas_call x1, Pallas kernels, fast_body(): pl.pallas_call(fast_kernel, out_shape=jax.ShapeDtypeStruct((mine, side, s...  44.4 us
    unnamed x1, local copies, waits for them, and re-layouts  1.77 us

profile of v3, /device:TPU:0, one launch (start us, length us, event | category | flops | bytes accessed | tf_op | source)
XLA Modules:
  0.0 47.5 jit_solution(14487747101292596116)
XLA Ops:
  1.3 44.4 %shard_map.73 = bf16[12,128,128]{2,1,0:T(8,128)(2,1)} custom-call(bf16[16,128,128]{2,1,0:T(8,128)(2,1)} %bitcast.11, bf16[8,128,128]{2,1,0:T(8,128)(2,1)} %bitcast.12, s32[16]{0:T(128)} %bitcast.13, s32[1]{0:T(128)} %bitcast.8.a_cnt, s32[8]{0:T(128)} %bitcast.14, s32[1]{0:T(128)} %bitcast.9.b_cnt, s32[24]{0:T(128)} %bitcast.15), custom_call_target="tpu_custom_call" | custom-call | flops 4294967296 | bytes 4194304 | tf_op jit(solution)/shard_map/pallas_call | solution.py:412
  45.7 1.8 %copy.11 = bf16[1,1,12,128,128]{4,3,2,1,0:T(8,128)(2,1)} copy(bf16[1,1,12,128,128]{4,3,2,1,0:T(8,128)(2,1)} %bitcast.10) | data formatting | bytes 786432

commit v4 on v3

--- a/solution.py
+++ b/solution.py
@@ -8,7 +8,7 @@
 RB = 4
 KB = 8
 CB = 8
-NCH = 4
+NCH = 8
 MESH = pl.DeviceIdType.MESH
 
 

time: 47.6 us -> 48.3 us (1.015)
  Pallas kernels: 44.4 us -> 45.1 us
    pallas_call x1, Pallas kernels: 44.4 us -> 45.1 us  [fast_body(): pl.pallas_call(fast_kernel, out_shape=jax.ShapeDtypeStruct((mine, side, s...]
where the time goes in v4:
time: 48.3 us; the launch traced here: 48.1 us
  Pallas kernels  45.1 us (93%)
  local copies, waits for them, and re-layouts  1.77 us (4%)
  between operations  1.3 us (3%)
    pallas_call x1, Pallas kernels, fast_body(): pl.pallas_call(fast_kernel, out_shape=jax.ShapeDtypeStruct((mine, side, s...  45.1 us
    unnamed x1, local copies, waits for them, and re-layouts  1.77 us

profile of v4, /device:TPU:0, one launch (start us, length us, event | category | flops | bytes accessed | tf_op | source)
XLA Modules:
  0.0 48.1 jit_solution(17350410493441940708)
XLA Ops:
  1.3 45.1 %shard_map.73 = bf16[12,128,128]{2,1,0:T(8,128)(2,1)} custom-call(bf16[16,128,128]{2,1,0:T(8,128)(2,1)} %bitcast.11, bf16[8,128,128]{2,1,0:T(8,128)(2,1)} %bitcast.12, s32[16]{0:T(128)} %bitcast.13, s32[1]{0:T(128)} %bitcast.8.a_cnt, s32[8]{0:T(128)} %bitcast.14, s32[1]{0:T(128)} %bitcast.9.b_cnt, s32[24]{0:T(128)} %bitcast.15), custom_call_target="tpu_custom_call" | custom-call | flops 4294967296 | bytes 4194304 | tf_op jit(solution)/shard_map/pallas_call | solution.py:412
  46.4 1.8 %copy.11 = bf16[1,1,12,128,128]{4,3,2,1,0:T(8,128)(2,1)} copy(bf16[1,1,12,128,128]{4,3,2,1,0:T(8,128)(2,1)} %bitcast.10) | data formatting | bytes 786432
